TPU v7x, 32 devices: a whole 2x2x4 slice. The times are simulated.
32 devices in a mesh: groups: 2 (over y), ra: 4 (over z), dec: 2 (over x), band: 2 (over core).
Axes of the slice: x: 2, y: 2, z: 4, core: 2. Of those that a mesh axis runs over, the one named last changes fastest.
Arguments:
- sky_maps: bfloat16 [512, 312, 256], P(('groups', 'band'), 'ra', 'dec'), parts along dimension 0, may hold values from -12 to 12
- radii: int32 [512], P(('groups', 'band')), parts along dimension 0, may hold values from 1 to 17, as said below
- valid: int32 [624, 256], P(('groups', 'ra'), 'dec'), parts along dimension 0, may hold values from 0 to 1, as said below
Outputs:
- smoothed: bfloat16 [512, 312, 256], P(('groups', 'band'), 'ra', 'dec'), parts along dimension 0
- channel_mean: float32 [512], P(('groups', 'band')), parts along dimension 0
- covariance: float32 [512, 256], P('groups', 'band'), parts along dimension 0
There are 2 independent parts, one for each index of `groups`. A program takes and returns all parts, laid end to end along the dimension named above; each array names one. Nothing has to cross between parts.
Inputs may be any that keep to these rules, and one draw needn't show every extreme that they name: `radii`: some channel has half-width exactly 17. 1 marks a pixel that enters the statistics; the pixel with declination index 0 is valid in every row.
All inputs are finite; a program needn't handle non-finite values.
Results may differ from a plain program's by a relative error of at most 0.012.
The roundings to bfloat16 on the way count: a program that leaves them out, or rounds other values in their place, can miss the bound.
Values may be sent and summed in bfloat16 or wider, within the bound.
A program may use at most 64 MiB of HBM per device.

v0:
```python
import jax
import jax.numpy as jnp
from jax import lax
from jax.sharding import PartitionSpec as P

RMAX = 17


def extended(array, sides, width, wrap):
    for axis, dim in sides:
        peers, length = (lax.axis_size(axis), array.shape[dim])
        up = [(i, (i + 1) % peers) for i in range(peers if wrap else peers - 1)]
        down = [(j, i) for i, j in up]
        last = lax.slice_in_dim(array, length - width, length, axis=dim)
        initial = lax.slice_in_dim(array, 0, width, axis=dim)
        before = lax.ppermute(last, axis, up)
        after = lax.ppermute(initial, axis, down)
        array = jnp.concatenate([before, array, after], axis=dim)
    return array


def beam_taps(radii, offsets):
    radius = radii.astype(jnp.float32)
    lead_shape = (radii.shape[0],) + (1,) * offsets.ndim
    radius = radius.reshape(lead_shape)
    spread = 0.5 * radius
    inside = jnp.abs(offsets)[None] <= radius
    return jnp.where(inside, jnp.exp(-(offsets * offsets)[None] / (2.0 * spread * spread)), 0.0)


def banded(radii, inner_count, outer_count):
    raw_taps = beam_taps(radii, jnp.arange(-RMAX, RMAX + 1).astype(jnp.float32))
    tap_total = jnp.sum(raw_taps, axis=1)
    offsets = (
        lax.broadcasted_iota(jnp.int32, (inner_count, outer_count), 0)
        - lax.broadcasted_iota(jnp.int32, (inner_count, outer_count), 1)
        - RMAX
    ).astype(jnp.float32)
    return (beam_taps(radii, offsets) / tap_total[:, None, None]).astype(jnp.bfloat16)


def local_sums(maps, mask_values):
    flat = maps.reshape(maps.shape[0], -1)
    weights = mask_values.reshape(-1)
    masked = flat * weights.astype(jnp.bfloat16)[None]
    sums = jnp.sum(masked.astype(jnp.float32), axis=1)
    return (masked, sums, jnp.sum(weights))


def per_device(sky_maps, radii, valid):
    channel_count, pixel_rows, pixel_cols = sky_maps.shape
    dec_band = banded(radii, pixel_cols + 2 * RMAX, pixel_cols)
    ra_band = banded(radii, pixel_rows + 2 * RMAX, pixel_rows)
    wrapped = extended(sky_maps, (("ra", 1),), RMAX, True)
    framed = extended(wrapped, (("dec", 2),), RMAX, False)
    across = jnp.einsum(
        "cxz,czy->cxy", framed, dec_band, preferred_element_type=jnp.float32
    ).astype(jnp.bfloat16)
    smoothed = jnp.einsum(
        "czy,czw->cwy", across, ra_band, preferred_element_type=jnp.float32
    ).astype(jnp.bfloat16)
    mask_values = valid.astype(jnp.float32)
    first_channel = lax.axis_index("band") * channel_count
    every = lax.all_gather(smoothed, "band", axis=0, tiled=True)
    masked, sums, count = local_sums(every, mask_values)
    own_rows = lax.dynamic_slice_in_dim(masked, first_channel, channel_count, 0)
    block = lax.dot_general(
        masked, own_rows, (((1,), (1,)), ((), ())), preferred_element_type=jnp.float32
    )
    sums, count, block = lax.psum((sums, count, block), ("ra", "dec"))
    mean_all = sums / count
    channel_mean = lax.dynamic_slice_in_dim(mean_all, first_channel, channel_count, 0)
    covariance = (block - count * mean_all[:, None] * channel_mean[None, :]) / (count - 1.0)
    return (smoothed, channel_mean, covariance)


def solution(mesh):
    return jax.shard_map(
        per_device,
        mesh=mesh,
        in_specs=(
            P(("groups", "band"), "ra", "dec"),
            P(("groups", "band")),
            P(("groups", "ra"), "dec"),
        ),
        out_specs=(P(("groups", "band"), "ra", "dec"), P(("groups", "band")), P("groups", "band")),
        check_vma=False,
    )
```

profile of v0, /device:TPU:0, one launch (start us, length us, event | category | flops | bytes accessed | tf_op | source)
XLA Modules:
  0.0 190.9 jit_solution(9157227778549513392)
XLA Ops:
  7.2 1.3 fusion.54
  8.5 3.1 %collective-permute-start = (bf16[128,17,128]{2,0,1:T(8,128)(2,1)S(1)}, bf16[128,17,128]{2,0,1:T(8,128)(2,1)S(1)}, u32[]{:S(2)}, u32[]{:S(2)}) collective-permute-start(bf16[128,17,128]{2,0,1:T(8,128)(2,1)S(1)} %get-tuple-element.24), channel_id=1, source_target_pairs={{0,4},{4,8},{8,12},{12,0},{1,5},{5,9},{9,13},{13,1},{2,6},{6,10},{... | collective-permute-start | bytes 1671176 | tf_op jit(solution)/shard_map/ppermute | solution.py:16
  11.6 2.1 %collective-permute-start.1 = (bf16[128,17,128]{2,0,1:T(8,128)(2,1)S(1)}, bf16[128,17,128]{2,0,1:T(8,128)(2,1)S(1)}, u32[]{:S(2)}, u32[]{:S(2)}) collective-permute-start(bf16[128,17,128]{2,0,1:T(8,128)(2,1)S(1)} %get-tuple-element.25), channel_id=1, source_target_pairs={{4,0},{8,4},{12,8},{0,12},{5,1},{9,5},{13,9},{1,13},{6,2},{10,6},{... | collective-permute-start | bytes 1671176 | tf_op jit(solution)/shard_map/ppermute | solution.py:17
  13.7 6.1 %copy.30 = bf16[128,78,128]{1,2,0:T(8,128)(2,1)} copy(bf16[128,78,128]{2,0,1:T(8,128)(2,1)} %param.3) | data formatting | bytes 5111808 | tf_op args[0]
  20.5 6.7 %collective-permute-done = bf16[128,17,128]{2,0,1:T(8,128)(2,1)S(1)} collective-permute-done((bf16[128,17,128]{2,0,1:T(8,128)(2,1)S(1)}, bf16[128,17,128]{2,0,1:T(8,128)(2,1)S(1)}, u32[]{:S(2)}, u32[]{:S(2)}) %collective-permute-start) | collective-permute-done | bytes 557088 | tf_op jit(solution)/shard_map/ppermute | solution.py:16
  27.1 3.3 %copy.29 = bf16[128,17,128]{1,2,0:T(8,128)(2,1)} copy(bf16[128,17,128]{2,0,1:T(8,128)(2,1)S(1)} %collective-permute-done) | data formatting | bytes 1114112 | tf_op jit(solution)/shard_map/ppermute | solution.py:16
  30.4 7.2 %collective-permute-done.1 = bf16[128,17,128]{2,0,1:T(8,128)(2,1)S(1)} collective-permute-done((bf16[128,17,128]{2,0,1:T(8,128)(2,1)S(1)}, bf16[128,17,128]{2,0,1:T(8,128)(2,1)S(1)}, u32[]{:S(2)}, u32[]{:S(2)}) %collective-permute-start.1) | collective-permute-done | bytes 557088 | tf_op jit(solution)/shard_map/ppermute | solution.py:17
  37.6 3.3 %copy.31 = bf16[128,17,128]{1,2,0:T(8,128)(2,1)} copy(bf16[128,17,128]{2,0,1:T(8,128)(2,1)S(1)} %collective-permute-done.1) | data formatting | bytes 1114112 | tf_op jit(solution)/shard_map/ppermute | solution.py:17
  40.9 4.2 %pad_maximum_fusion.2 = (bf16[128,112,17]{1,2,0:T(8,128)(2,1)S(1)}, bf16[128,112,17]{1,2,0:T(8,128)(2,1)S(1)}) fusion(bf16[128,17,128]{1,2,0:T(8,128)(2,1)} %copy.31, bf16[128,78,128]{1,2,0:T(8,128)(2,1)} %copy.30, bf16[128,17,128]{1,2,0:T(8,128)(2,1)} %copy.29), kind=kLoop, calls=%fused_computation.39 | loop fusion | flops 2924544 | bytes 4644864 | tf_op jit(solution)/shard_map/slice | solution.py:14
  45.5 3.4 %collective-permute-start.2 = (bf16[128,112,17]{0,1,2:T(8,128)(2,1)S(1)}, bf16[128,112,17]{0,1,2:T(8,128)(2,1)S(1)}, u32[]{:S(2)}, u32[]{:S(2)}) collective-permute-start(bf16[128,112,17]{0,1,2:T(8,128)(2,1)S(1)} %copy.32), channel_id=1, source_target_pairs={{0,2},{1,3},{4,6},{5,7},{8,10},{9,11},{12,14},{13,15},{16,18},{17,... | collective-permute-start | bytes 1462280 | tf_op jit(solution)/shard_map/ppermute | solution.py:16
  49.4 1.3 collective-permute-start.3
  51.5 7.3 %collective-permute-done.2 = bf16[128,112,17]{0,1,2:T(8,128)(2,1)S(1)} collective-permute-done((bf16[128,112,17]{0,1,2:T(8,128)(2,1)S(1)}, bf16[128,112,17]{0,1,2:T(8,128)(2,1)S(1)}, u32[]{:S(2)}, u32[]{:S(2)}) %collective-permute-start.2) | collective-permute-done | bytes 487456 | tf_op jit(solution)/shard_map/ppermute | solution.py:16
  59.3 4.2 %collective-permute-done.3 = bf16[128,112,17]{0,1,2:T(8,128)(2,1)S(1)} collective-permute-done((bf16[128,112,17]{0,1,2:T(8,128)(2,1)S(1)}, bf16[128,112,17]{0,1,2:T(8,128)(2,1)S(1)}, u32[]{:S(2)}, u32[]{:S(2)}) %collective-permute-start.3) | collective-permute-done | bytes 487456 | tf_op jit(solution)/shard_map/ppermute | solution.py:17
  63.5 1.2 copy.35
  64.7 13.9 %fusion.34 = bf16[128,78,128]{2,1,0:T(8,128)(2,1)S(1)} fusion(f32[128]{0:T(128)S(1)} %fusion.48, f32[128]{0:T(128)S(1)} %multiply_multiply_fusion, f32[112,78]{0,1:T(8,128)S(1)} %get-tuple-element.30, f32[112,78]{0,1:T(8,128)} %get-tuple-element.31, f32[128]{0:T(128)S(1)} %convert_element_type.74, bf16[128,112,17]{1,2,0:T(8,128)(2,1)} %copy.35, ...), kind=kOutput, calls=%fused_computation.36 | convolution fusion | flops 926003200 | bytes 7438080 | tf_op jit(solution)/shard_map/czy,czw->cwy/dot_general | solution.py:59
  78.7 2.1 %copy.38 = bf16[128,78,128]{2,0,1:T(8,128)(2,1)} copy(bf16[128,78,128]{2,1,0:T(8,128)(2,1)S(1)} %fusion.34) | data formatting | bytes 5111808
  81.7 13.3 %all-gather.2.cloned.1.call-done = bf16[256,78,128]{2,0,1:T(8,128)(2,1)} async-done(((bf16[128,78,128]{2,0,1:T(8,128)(2,1)}), bf16[256,78,128]{2,0,1:T(8,128)(2,1)}) %all-gather.2.cloned.1.call-update) | async-done | bytes 5111824 | tf_op jit(solution)/shard_map/all_gather | solution.py:64
  95.0 7.7 %copy.37 = bf16[256,78,128]{0,2,1:T(8,128)(2,1)} copy(bf16[256,78,128]{2,0,1:T(8,128)(2,1)} %all-gather.2.cloned.1.call-done) | data formatting | bytes 10223616 | tf_op jit(solution)/shard_map/all_gather | solution.py:64
  102.8 6.3 %bitcast_multiply_fusion = bf16[256,9984]{0,1:T(8,128)(2,1)S(1)} fusion(bf16[256,78,128]{0,2,1:T(8,128)(2,1)} %copy.37, bf16[9984]{0:T(1024)(128)(2,1)S(1)} %fusion.56), kind=kLoop, calls=%fused_computation.25 | loop fusion | flops 2555904 | bytes 10243584 | tf_op jit(solution)/shard_map/mul | solution.py:45
  109.0 2.3 %fusion.32 = f32[256,128]{1,0:T(8,128)} fusion(bf16[256,9984]{0,1:T(8,128)(2,1)S(1)} %bitcast_multiply_fusion, s32[]{:T(128)S(6)} %select_n.20), kind=kOutput, calls=%fused_computation.34 | convolution fusion | flops 654311424 | bytes 7798788 | tf_op jit(solution)/shard_map/dot_general | solution.py:67
  111.3 3.7 %convert_reduce_fusion = f32[256]{0:T(256)S(1)} fusion(bf16[256,78,128]{2,0,1:T(8,128)(2,1)} %all-gather.2.cloned.1.call-done, bf16[78,128]{1,0:T(8,128)(2,1)S(1)} %convert_convert_fusion), kind=kLoop, calls=%fused_computation.4 | loop fusion | flops 7667456 | bytes 5132800 | tf_op jit(solution)/shard_map/reduce_sum | solution.py:46
  115.0 22.4 %all-reduce = (f32[256]{0:T(256)S(1)}, f32[]{:T(128)}) all-reduce(f32[256]{0:T(256)S(1)} %convert_reduce_fusion, f32[]{:T(128)} %convert_reduce_fusion.1), channel_id=1, replica_groups=mesh['groups'=2,'ra'=4,'dec'=2,'band'=2] {'ra','dec'}, use_global_device_ids=true, to_apply=%region_2.3 | all-reduce | flops 257 | bytes 2056 | tf_op jit(solution)/shard_map/psum | solution.py:70
  138.6 43.8 %all-reduce.3.cloned.1.call-done = f32[256,128]{1,0:T(8,128)} async-done(((f32[256,128]{1,0:T(8,128)}), f32[256,128]{1,0:T(8,128)}) %all-reduce.3.cloned.1.call-update) | async-done | bytes 131088 | tf_op jit(solution)/shard_map/psum | solution.py:70
  182.3 1.7 subtract_divide_fusion
  (24 shorter events, 4.3 us)
Async XLA Ops:
  7.2 87.9 %all-gather.2.cloned.1.call-start = ((), (), s32[]{:S(2)}) async-start(), calls=%async_computation | async-start | bytes 7667712 | tf_op jit(solution)/shard_map/all_gather | solution.py:64
  8.5 18.6 %collective-permute-start = (bf16[128,17,128]{2,0,1:T(8,128)(2,1)S(1)}, bf16[128,17,128]{2,0,1:T(8,128)(2,1)S(1)}, u32[]{:S(2)}, u32[]{:S(2)}) collective-permute-start(bf16[128,17,128]{2,0,1:T(8,128)(2,1)S(1)} %get-tuple-element.24), channel_id=1, source_target_pairs={{0,4},{4,8},{8,12},{12,0},{1,5},{5,9},{9,13},{13,1},{2,6},{6,10},{... | collective-permute-start | bytes 1671176 | tf_op jit(solution)/shard_map/ppermute | solution.py:16
  11.6 26.0 %collective-permute-start.1 = (bf16[128,17,128]{2,0,1:T(8,128)(2,1)S(1)}, bf16[128,17,128]{2,0,1:T(8,128)(2,1)S(1)}, u32[]{:S(2)}, u32[]{:S(2)}) collective-permute-start(bf16[128,17,128]{2,0,1:T(8,128)(2,1)S(1)} %get-tuple-element.25), channel_id=1, source_target_pairs={{4,0},{8,4},{12,8},{0,12},{5,1},{9,5},{13,9},{1,13},{6,2},{10,6},{... | collective-permute-start | bytes 1671176 | tf_op jit(solution)/shard_map/ppermute | solution.py:17
  40.9 9.9 %copy-start.2 = (s32[128]{0:T(128)S(1)}, s32[128]{0:T(128)}, u32[]{:S(2)}) copy-start(s32[128]{0:T(128)} %param.4) | copy-start | bytes 1540
  45.5 13.3 %collective-permute-start.2 = (bf16[128,112,17]{0,1,2:T(8,128)(2,1)S(1)}, bf16[128,112,17]{0,1,2:T(8,128)(2,1)S(1)}, u32[]{:S(2)}, u32[]{:S(2)}) collective-permute-start(bf16[128,112,17]{0,1,2:T(8,128)(2,1)S(1)} %copy.32), channel_id=1, source_target_pairs={{0,2},{1,3},{4,6},{5,7},{8,10},{9,11},{12,14},{13,15},{16,18},{17,... | collective-permute-start | bytes 1462280 | tf_op jit(solution)/shard_map/ppermute | solution.py:16
  49.4 14.0 %collective-permute-start.3 = (bf16[128,112,17]{0,1,2:T(8,128)(2,1)S(1)}, bf16[128,112,17]{0,1,2:T(8,128)(2,1)S(1)}, u32[]{:S(2)}, u32[]{:S(2)}) collective-permute-start(bf16[128,112,17]{0,1,2:T(8,128)(2,1)S(1)} %copy.33), channel_id=1, source_target_pairs={{2,0},{3,1},{6,4},{7,5},{10,8},{11,9},{14,12},{15,13},{18,16},{19,... | collective-permute-start | bytes 1462280 | tf_op jit(solution)/shard_map/ppermute | solution.py:17
  78.7 2.4 %copy-start = (s32[78,128]{1,0:T(8,128)S(1)}, s32[78,128]{1,0:T(8,128)}, u32[]{:S(2)}) copy-start(s32[78,128]{1,0:T(8,128)} %param.5) | copy-start | bytes 119812
  80.9 101.5 %all-reduce.3.cloned.1.call-start = ((), (), s32[]{:S(2)}) async-start(), calls=%async_computation.1 | async-start | bytes 262144 | tf_op jit(solution)/shard_map/psum | solution.py:70
  138.0 46.0 %copy-start.1 = (f32[128]{0:T(128)}, f32[128]{0:T(128)S(1)}, u32[]{:S(2)}) copy-start(f32[128]{0:T(128)S(1)} %dynamic_slice.6) | copy-start | bytes 1540
Sparse Core Ops, SparseCore 0:
  81.0 13.9 all-gather.1
  111.4 70.8 all-reduce.2
where the time goes:
time: 191 us
  waiting for transfers between devices  82.4 us (43%)
  local copies, waits for them, and re-layouts  26.6 us (14%)
  blocking collectives  22.4 us (12%)
  other arithmetic  18.3 us (10%)
  matrix products  16.2 us (8%)
  between operations  14.7 us (8%)
  starting transfers between devices  10.1 us (5%)
    psum x1, waiting for transfers between devices, per_device(): sums, count, block = lax.psum((sums, count, block), ('ra', 'dec'))  43.8 us
    psum x1, blocking collectives, per_device(): sums, count, block = lax.psum((sums, count, block), ('ra', 'dec'))  22.4 us
    ppermute x2, waiting for transfers between devices, extended(): before = lax.ppermute(last, axis, up)  14 us
    dot_general x1, matrix products, per_device(): jnp.einsum('czy,czw->cwy', across, ra_band, preferred_element_type=jnp.fl...  13.9 us
    all_gather x1, waiting for transfers between devices, per_device(): every = lax.all_gather(smoothed, 'band', axis=0, tiled=True)  13.3 us
    ppermute x2, waiting for transfers between devices, extended(): after = lax.ppermute(initial, axis, down)  11.4 us
    unnamed x8, local copies, waits for them, and re-layouts  8.3 us
    all_gather x1, local copies, waits for them, and re-layouts, per_device(): every = lax.all_gather(smoothed, 'band', axis=0, tiled=True)  7.73 us
  transfers between devices with their start and end apart: 6, of which 6 were waited for; matrix products, arithmetic and copies ran while one was open for 9% of the time, Pallas kernels for 0%

commit v1 on v0

--- a/solution.py
+++ b/solution.py
@@ -67,7 +67,7 @@
     block = lax.dot_general(
         masked, own_rows, (((1,), (1,)), ((), ())), preferred_element_type=jnp.float32
     )
-    sums, count, block = lax.psum((sums, count, block), ("ra", "dec"))
+    sums, count, block = lax.psum(lax.psum((sums, count, block), "dec"), "ra")
     mean_all = sums / count
     channel_mean = lax.dynamic_slice_in_dim(mean_all, first_channel, channel_count, 0)
     covariance = (block - count * mean_all[:, None] * channel_mean[None, :]) / (count - 1.0)

time: 191 us -> 180 us (0.942)
  waiting for transfers between devices: 82.4 us -> 75 us
  blocking collectives: 22.4 us -> 18.2 us
    psum x1 -> x2, waiting for transfers between devices: 43.8 us -> 36.4 us  [per_device(): sums, count, block = lax.psum(lax.psum((sums, count, block), 'dec'), 'ra')]
    psum x1 -> x2, blocking collectives: 22.4 us -> 18.2 us  [per_device(): sums, count, block = lax.psum(lax.psum((sums, count, block), 'dec'), 'ra')]
  transfers between devices with their start and end apart: 6 -> 7, of which waited for: 6 -> 7; matrix products, arithmetic and copies ran while one was open for 9% -> 9% of each run, Pallas kernels for 0% -> 0%
where the time goes in v1:
time: 180 us; the launch traced here: 179 us
  waiting for transfers between devices  75 us (42%)
  local copies, waits for them, and re-layouts  26.6 us (15%)
  other arithmetic  18.4 us (10%)
  blocking collectives  18.2 us (10%)
  matrix products  16.2 us (9%)
  between operations  14.5 us (8%)
  starting transfers between devices  10.2 us (6%)
    psum x2, waiting for transfers between devices, per_device(): sums, count, block = lax.psum(lax.psum((sums, count, block), 'dec'), 'ra')  36.4 us
    psum x2, blocking collectives, per_device(): sums, count, block = lax.psum(lax.psum((sums, count, block), 'dec'), 'ra')  18.2 us
    ppermute x2, waiting for transfers between devices, extended(): before = lax.ppermute(last, axis, up)  14 us
    dot_general x1, matrix products, per_device(): jnp.einsum('czy,czw->cwy', across, ra_band, preferred_element_type=jnp.fl...  13.9 us
    all_gather x1, waiting for transfers between devices, per_device(): every = lax.all_gather(smoothed, 'band', axis=0, tiled=True)  13.3 us
    ppermute x2, waiting for transfers between devices, extended(): after = lax.ppermute(initial, axis, down)  11.4 us
    unnamed x8, local copies, waits for them, and re-layouts  8.3 us
    all_gather x1, local copies, waits for them, and re-layouts, per_device(): every = lax.all_gather(smoothed, 'band', axis=0, tiled=True)  7.74 us
  transfers between devices with their start and end apart: 7, of which 7 were waited for; matrix products, arithmetic and copies ran while one was open for 9% of the time, Pallas kernels for 0%

profile of v1, /device:TPU:0, one launch (start us, length us, event | category | flops | bytes accessed | tf_op | source)
XLA Modules:
  0.0 179.2 jit_solution(224410944097852753)
XLA Ops:
  7.2 1.3 fusion.54
  8.5 3.1 %collective-permute-start = (bf16[128,17,128]{2,0,1:T(8,128)(2,1)S(1)}, bf16[128,17,128]{2,0,1:T(8,128)(2,1)S(1)}, u32[]{:S(2)}, u32[]{:S(2)}) collective-permute-start(bf16[128,17,128]{2,0,1:T(8,128)(2,1)S(1)} %get-tuple-element.26), channel_id=1, source_target_pairs={{0,4},{4,8},{8,12},{12,0},{1,5},{5,9},{9,13},{13,1},{2,6},{6,10},{... | collective-permute-start | bytes 1671176 | tf_op jit(solution)/shard_map/ppermute | solution.py:16
  11.6 2.1 %collective-permute-start.1 = (bf16[128,17,128]{2,0,1:T(8,128)(2,1)S(1)}, bf16[128,17,128]{2,0,1:T(8,128)(2,1)S(1)}, u32[]{:S(2)}, u32[]{:S(2)}) collective-permute-start(bf16[128,17,128]{2,0,1:T(8,128)(2,1)S(1)} %get-tuple-element.27), channel_id=1, source_target_pairs={{4,0},{8,4},{12,8},{0,12},{5,1},{9,5},{13,9},{1,13},{6,2},{10,6},{... | collective-permute-start | bytes 1671176 | tf_op jit(solution)/shard_map/ppermute | solution.py:17
  13.7 6.2 %copy.30 = bf16[128,78,128]{1,2,0:T(8,128)(2,1)} copy(bf16[128,78,128]{2,0,1:T(8,128)(2,1)} %param.3) | data formatting | bytes 5111808 | tf_op args[0]
  20.5 6.6 %collective-permute-done = bf16[128,17,128]{2,0,1:T(8,128)(2,1)S(1)} collective-permute-done((bf16[128,17,128]{2,0,1:T(8,128)(2,1)S(1)}, bf16[128,17,128]{2,0,1:T(8,128)(2,1)S(1)}, u32[]{:S(2)}, u32[]{:S(2)}) %collective-permute-start) | collective-permute-done | bytes 557088 | tf_op jit(solution)/shard_map/ppermute | solution.py:16
  27.1 3.3 %copy.29 = bf16[128,17,128]{1,2,0:T(8,128)(2,1)} copy(bf16[128,17,128]{2,0,1:T(8,128)(2,1)S(1)} %collective-permute-done) | data formatting | bytes 1114112 | tf_op jit(solution)/shard_map/ppermute | solution.py:16
  30.4 7.2 %collective-permute-done.1 = bf16[128,17,128]{2,0,1:T(8,128)(2,1)S(1)} collective-permute-done((bf16[128,17,128]{2,0,1:T(8,128)(2,1)S(1)}, bf16[128,17,128]{2,0,1:T(8,128)(2,1)S(1)}, u32[]{:S(2)}, u32[]{:S(2)}) %collective-permute-start.1) | collective-permute-done | bytes 557088 | tf_op jit(solution)/shard_map/ppermute | solution.py:17
  37.6 3.3 %copy.31 = bf16[128,17,128]{1,2,0:T(8,128)(2,1)} copy(bf16[128,17,128]{2,0,1:T(8,128)(2,1)S(1)} %collective-permute-done.1) | data formatting | bytes 1114112 | tf_op jit(solution)/shard_map/ppermute | solution.py:17
  40.9 4.2 %pad_maximum_fusion.2 = (bf16[128,112,17]{1,2,0:T(8,128)(2,1)S(1)}, bf16[128,112,17]{1,2,0:T(8,128)(2,1)S(1)}) fusion(bf16[128,17,128]{1,2,0:T(8,128)(2,1)} %copy.31, bf16[128,78,128]{1,2,0:T(8,128)(2,1)} %copy.30, bf16[128,17,128]{1,2,0:T(8,128)(2,1)} %copy.29), kind=kLoop, calls=%fused_computation.39 | loop fusion | flops 2924544 | bytes 4644864 | tf_op jit(solution)/shard_map/slice | solution.py:14
  45.5 3.4 %collective-permute-start.2 = (bf16[128,112,17]{0,1,2:T(8,128)(2,1)S(1)}, bf16[128,112,17]{0,1,2:T(8,128)(2,1)S(1)}, u32[]{:S(2)}, u32[]{:S(2)}) collective-permute-start(bf16[128,112,17]{0,1,2:T(8,128)(2,1)S(1)} %copy.32), channel_id=1, source_target_pairs={{0,2},{1,3},{4,6},{5,7},{8,10},{9,11},{12,14},{13,15},{16,18},{17,... | collective-permute-start | bytes 1462280 | tf_op jit(solution)/shard_map/ppermute | solution.py:16
  49.4 1.3 collective-permute-start.3
  51.5 7.3 %collective-permute-done.2 = bf16[128,112,17]{0,1,2:T(8,128)(2,1)S(1)} collective-permute-done((bf16[128,112,17]{0,1,2:T(8,128)(2,1)S(1)}, bf16[128,112,17]{0,1,2:T(8,128)(2,1)S(1)}, u32[]{:S(2)}, u32[]{:S(2)}) %collective-permute-start.2) | collective-permute-done | bytes 487456 | tf_op jit(solution)/shard_map/ppermute | solution.py:16
  59.3 4.2 %collective-permute-done.3 = bf16[128,112,17]{0,1,2:T(8,128)(2,1)S(1)} collective-permute-done((bf16[128,112,17]{0,1,2:T(8,128)(2,1)S(1)}, bf16[128,112,17]{0,1,2:T(8,128)(2,1)S(1)}, u32[]{:S(2)}, u32[]{:S(2)}) %collective-permute-start.3) | collective-permute-done | bytes 487456 | tf_op jit(solution)/shard_map/ppermute | solution.py:17
  64.7 13.9 %fusion.34 = bf16[128,78,128]{2,1,0:T(8,128)(2,1)S(1)} fusion(f32[128]{0:T(128)S(1)} %fusion.48, f32[128]{0:T(128)S(1)} %multiply_multiply_fusion, f32[112,78]{0,1:T(8,128)S(1)} %get-tuple-element.32, f32[112,78]{0,1:T(8,128)} %get-tuple-element.33, f32[128]{0:T(128)S(1)} %convert_element_type.74, bf16[128,112,17]{1,2,0:T(8,128)(2,1)} %copy.35, ...), kind=kOutput, calls=%fused_computation.36 | convolution fusion | flops 926003200 | bytes 7438080 | tf_op jit(solution)/shard_map/czy,czw->cwy/dot_general | solution.py:59
  78.7 2.1 %copy.38 = bf16[128,78,128]{2,0,1:T(8,128)(2,1)} copy(bf16[128,78,128]{2,1,0:T(8,128)(2,1)S(1)} %fusion.34) | data formatting | bytes 5111808
  81.7 13.3 %all-gather.2.cloned.1.call-done = bf16[256,78,128]{2,0,1:T(8,128)(2,1)} async-done(((bf16[128,78,128]{2,0,1:T(8,128)(2,1)}), bf16[256,78,128]{2,0,1:T(8,128)(2,1)}) %all-gather.2.cloned.1.call-update) | async-done | bytes 5111824 | tf_op jit(solution)/shard_map/all_gather | solution.py:64
  95.0 7.7 %copy.37 = bf16[256,78,128]{0,2,1:T(8,128)(2,1)} copy(bf16[256,78,128]{2,0,1:T(8,128)(2,1)} %all-gather.2.cloned.1.call-done) | data formatting | bytes 10223616 | tf_op jit(solution)/shard_map/all_gather | solution.py:64
  102.8 6.3 %bitcast_multiply_fusion = bf16[256,9984]{0,1:T(8,128)(2,1)S(1)} fusion(bf16[256,78,128]{0,2,1:T(8,128)(2,1)} %copy.37, bf16[9984]{0:T(1024)(128)(2,1)S(1)} %fusion.56), kind=kLoop, calls=%fused_computation.25 | loop fusion | flops 2555904 | bytes 10243584 | tf_op jit(solution)/shard_map/mul | solution.py:45
  109.1 2.3 %fusion.32 = f32[256,128]{1,0:T(8,128)} fusion(bf16[256,9984]{0,1:T(8,128)(2,1)S(1)} %bitcast_multiply_fusion, s32[]{:T(128)S(6)} %select_n.20), kind=kOutput, calls=%fused_computation.34 | convolution fusion | flops 654311424 | bytes 7798788 | tf_op jit(solution)/shard_map/dot_general | solution.py:67
  111.4 3.7 %convert_reduce_fusion = f32[256]{0:T(256)S(1)} fusion(bf16[256,78,128]{2,0,1:T(8,128)(2,1)} %all-gather.2.cloned.1.call-done, bf16[78,128]{1,0:T(8,128)(2,1)S(1)} %convert_convert_fusion), kind=kLoop, calls=%fused_computation.4 | loop fusion | flops 7667456 | bytes 5132800 | tf_op jit(solution)/shard_map/reduce_sum | solution.py:46
  115.0 5.6 %all-reduce.1 = (f32[256]{0:T(256)S(1)}, f32[]{:T(128)}) all-reduce(f32[256]{0:T(256)S(1)} %convert_reduce_fusion, f32[]{:T(128)} %convert_reduce_fusion.1), channel_id=1, replica_groups=mesh['groups'=2,'ra'=4,'dec'=2,'band'=2] {'dec'}, use_global_device_ids=true, to_apply=%region_2.3 | all-reduce | flops 257 | bytes 2056 | tf_op jit(solution)/shard_map/psum | solution.py:70
  120.6 12.6 %all-reduce = (f32[256]{0:T(256)S(1)}, f32[]{:T(128)}) all-reduce(f32[256]{0:T(256)S(1)} %get-tuple-element.20, f32[]{:T(128)} %get-tuple-element.21), channel_id=1, replica_groups=mesh['groups'=2,'ra'=4,'dec'=2,'band'=2] {'ra'}, use_global_device_ids=true, to_apply=%region_3.4 | all-reduce | flops 257 | bytes 2056 | tf_op jit(solution)/shard_map/psum | solution.py:70
  135.6 35.4 %all-reduce.7.cloned.1.call-done = f32[256,128]{1,0:T(8,128)} async-done(((f32[256,128]{1,0:T(8,128)}), f32[256,128]{1,0:T(8,128)}) %all-reduce.7.cloned.1.call-update) | async-done | bytes 131088 | tf_op jit(solution)/shard_map/psum | solution.py:70
  171.0 1.7 subtract_divide_fusion
  (28 shorter events, 6.6 us)
Async XLA Ops:
  7.2 87.9 %all-gather.2.cloned.1.call-start = ((), (), s32[]{:S(2)}) async-start(), calls=%async_computation | async-start | bytes 7667712 | tf_op jit(solution)/shard_map/all_gather | solution.py:64
  8.5 18.6 %collective-permute-start = (bf16[128,17,128]{2,0,1:T(8,128)(2,1)S(1)}, bf16[128,17,128]{2,0,1:T(8,128)(2,1)S(1)}, u32[]{:S(2)}, u32[]{:S(2)}) collective-permute-start(bf16[128,17,128]{2,0,1:T(8,128)(2,1)S(1)} %get-tuple-element.26), channel_id=1, source_target_pairs={{0,4},{4,8},{8,12},{12,0},{1,5},{5,9},{9,13},{13,1},{2,6},{6,10},{... | collective-permute-start | bytes 1671176 | tf_op jit(solution)/shard_map/ppermute | solution.py:16
  11.6 26.0 %collective-permute-start.1 = (bf16[128,17,128]{2,0,1:T(8,128)(2,1)S(1)}, bf16[128,17,128]{2,0,1:T(8,128)(2,1)S(1)}, u32[]{:S(2)}, u32[]{:S(2)}) collective-permute-start(bf16[128,17,128]{2,0,1:T(8,128)(2,1)S(1)} %get-tuple-element.27), channel_id=1, source_target_pairs={{4,0},{8,4},{12,8},{0,12},{5,1},{9,5},{13,9},{1,13},{6,2},{10,6},{... | collective-permute-start | bytes 1671176 | tf_op jit(solution)/shard_map/ppermute | solution.py:17
  40.9 9.9 %copy-start.2 = (s32[128]{0:T(128)S(1)}, s32[128]{0:T(128)}, u32[]{:S(2)}) copy-start(s32[128]{0:T(128)} %param.4) | copy-start | bytes 1540
  45.5 13.3 %collective-permute-start.2 = (bf16[128,112,17]{0,1,2:T(8,128)(2,1)S(1)}, bf16[128,112,17]{0,1,2:T(8,128)(2,1)S(1)}, u32[]{:S(2)}, u32[]{:S(2)}) collective-permute-start(bf16[128,112,17]{0,1,2:T(8,128)(2,1)S(1)} %copy.32), channel_id=1, source_target_pairs={{0,2},{1,3},{4,6},{5,7},{8,10},{9,11},{12,14},{13,15},{16,18},{17,... | collective-permute-start | bytes 1462280 | tf_op jit(solution)/shard_map/ppermute | solution.py:16
  49.4 14.0 %collective-permute-start.3 = (bf16[128,112,17]{0,1,2:T(8,128)(2,1)S(1)}, bf16[128,112,17]{0,1,2:T(8,128)(2,1)S(1)}, u32[]{:S(2)}, u32[]{:S(2)}) collective-permute-start(bf16[128,112,17]{0,1,2:T(8,128)(2,1)S(1)} %copy.33), channel_id=1, source_target_pairs={{2,0},{3,1},{6,4},{7,5},{10,8},{11,9},{14,12},{15,13},{18,16},{19,... | collective-permute-start | bytes 1462280 | tf_op jit(solution)/shard_map/ppermute | solution.py:17
  78.7 2.4 %copy-start = (s32[78,128]{1,0:T(8,128)S(1)}, s32[78,128]{1,0:T(8,128)}, u32[]{:S(2)}) copy-start(s32[78,128]{1,0:T(8,128)} %param.5) | copy-start | bytes 119812
  80.9 53.3 %all-reduce.5.cloned.1.call-start = ((), (), s32[]{:S(2)}) async-start(), calls=%async_computation.1 | async-start | bytes 262144 | tf_op jit(solution)/shard_map/psum | solution.py:70
  111.3 59.6 %all-reduce.7.cloned.1.call-start = ((), (), s32[]{:S(2)}) async-start(), calls=%async_computation.2 | async-start | bytes 262144 | tf_op jit(solution)/shard_map/psum | solution.py:70
  134.9 37.7 %copy-start.1 = (f32[128]{0:T(128)}, f32[128]{0:T(128)S(1)}, u32[]{:S(2)}) copy-start(f32[128]{0:T(128)S(1)} %dynamic_slice.6) | copy-start | bytes 1540
Sparse Core Ops, SparseCore 0:
  81.0 13.9 all-gather.1
  111.5 22.6 all-reduce.4
  136.5 34.4 all-reduce.6
